TPU v7x, 512 devices: a whole 4x4x16 slice. The times are simulated.
512 devices in a mesh: rep: 32 (over z, core), fsdp: 8 (over y, x_lo), tp: 2 (over x_hi).
Axes of the slice: x: 4 (x_hi: 2, x_lo: 2; x = x_hi * 2 + x_lo), y: 4, z: 16, core: 2. Of those that a mesh axis runs over, the one named last changes fastest.
Arguments:
- tokens: bfloat16 [32, 2, 5120, 512], P('rep', None, ('fsdp', 'tp')), may hold values from -6 to 6
- queries: bfloat16 [32, 2, 512, 4096], P('rep', None, 'fsdp', 'tp'), may hold values from -6 to 6
- cotangent: bfloat16 [32, 2, 512, 4096], P('rep', None, 'fsdp', 'tp'), may hold values from -6 to 6
- outer_weights: bfloat16 [32, 5120, 1024], P('rep', ('fsdp', 'tp')), may hold values from -4 to 4
- momentum: bfloat16 [32, 5120, 1024], P('rep', ('fsdp', 'tp')), may hold values from -3 to 3
- partner_mask: int32 [1], replicated, may hold values from 1 to 31
Outputs:
- new_weights: bfloat16 [32, 5120, 1024], P('rep', ('fsdp', 'tp'))
- new_momentum: bfloat16 [32, 5120, 1024], P('rep', ('fsdp', 'tp'))
Inputs may be any that keep to these rules, and one draw needn't show every extreme that they name: `partner_mask`: replica r is paired with replica r XOR the mask.
All inputs are finite; a program needn't handle non-finite values.
Results may differ from a plain program's by a relative error of at most 0.03.
Values may be sent and summed in bfloat16 or wider, within the bound.
A program may use at most 64 MiB of HBM per device.

v0:
```python
import jax
import jax.numpy as jnp
from jax import lax
from jax.sharding import PartitionSpec as P

D = 5120
HD = 128
KVH = 4
GROUP = 8
STEPS = 2


EPSILON = 1e-06
INNER_RATE = 8.0
MOMENTUM_DECAY = 0.9
DELTA_WEIGHT = 0.35
PAIR_WEIGHT = 0.25


def from_partner(value, axis, stride):
    mask = 2**stride
    pairs = [(source, source ^ mask) for source in range(lax.axis_size(axis))]
    return lax.ppermute(value, axis, pairs)


def column_scale(columns, model_width):
    half_cols = columns // 2
    return jnp.concatenate(
        [
            jnp.ones((half_cols,), jnp.float32),
            jnp.full((half_cols,), model_width ** (-0.5), jnp.float32),
        ]
    )


def block_gradient(key_values, queries, cotangent, first_row):
    seq_len = key_values.shape[0]
    query_rows, groups, key_heads, head_size = queries.shape
    key_cols = key_heads * head_size
    key_full = key_values[:, :key_cols].astype(jnp.float32).reshape(seq_len, key_heads, head_size)
    value_low = key_values[:, key_cols:].reshape(seq_len, key_heads, head_size)
    key_norm = lax.rsqrt(jnp.mean(key_full * key_full, axis=-1, keepdims=True) + EPSILON)
    key_unit = key_full * key_norm
    key_low = key_unit.astype(jnp.bfloat16)
    query_full = queries.astype(jnp.float32)
    query_low = (
        query_full * lax.rsqrt(jnp.mean(query_full * query_full, axis=-1, keepdims=True) + EPSILON)
    ).astype(jnp.bfloat16)
    scores = jnp.einsum(
        "rgkd,skd->kgrs", query_low, key_low, preferred_element_type=jnp.float32
    ) * head_size ** (-0.5)
    position = first_row + jnp.arange(query_rows, dtype=jnp.int32)
    allowed = jnp.arange(seq_len, dtype=jnp.int32)[None, :] <= position[:, None]
    raised = jnp.where(allowed, jnp.exp(scores), 0.0)
    attention = raised / jnp.sum(raised, axis=-1, keepdims=True)
    attention_low = attention.astype(jnp.bfloat16)
    value_part = jnp.einsum(
        "kgrs,rgkd->skd", attention_low, cotangent, preferred_element_type=jnp.float32
    )
    prob_grad = jnp.einsum(
        "rgkd,skd->kgrs", cotangent, value_low, preferred_element_type=jnp.float32
    )
    score_grad = attention * (prob_grad - jnp.sum(attention * prob_grad, axis=-1, keepdims=True))
    score_low = (score_grad * head_size ** (-0.5)).astype(jnp.bfloat16)
    unit_grad = jnp.einsum(
        "kgrs,rgkd->skd", score_low, query_low, preferred_element_type=jnp.float32
    )
    key_part = (
        unit_grad - key_unit * jnp.mean(unit_grad * key_unit, axis=-1, keepdims=True)
    ) * key_norm
    return jnp.concatenate(
        [key_part.reshape(seq_len, key_cols), value_part.reshape(seq_len, key_cols)], axis=1
    )


def partner_value(payload, mask_value, bit_count, hop):
    for bit_index in range(bit_count):
        moved = hop(payload, bit_index)
        chosen = jnp.bitwise_and(jnp.right_shift(mask_value, bit_index), 1) == 1
        payload = jnp.where(chosen, moved, payload)
    return payload


def on_device(tokens, queries, cotangent, outer_weights, momentum, partner_mask):
    features_all = tokens[0]
    query_all = queries[0]
    cotangent_all = cotangent[0]
    weights_low = outer_weights[0]
    momentum_low = momentum[0]
    mask_value = partner_mask[0]
    bit_count = lax.axis_size("rep").bit_length() - 1
    local_groups = GROUP // lax.axis_size("tp")
    query_rows = query_all.shape[1]
    first_row = lax.axis_index("fsdp") * query_rows
    columns = weights_low.shape[1]
    scale = column_scale(columns, D)
    inner = weights_low.astype(jnp.float32)
    for inner_step in range(STEPS):
        features = features_all[inner_step]
        inner_low = inner.astype(jnp.bfloat16)
        partial_value = lax.dot_general(
            features, inner_low, (((0,), (0,)), ((), ())), preferred_element_type=jnp.float32
        )
        key_values = (
            lax.psum(partial_value.astype(jnp.bfloat16), ("fsdp", "tp")).astype(jnp.float32) * scale
        ).astype(jnp.bfloat16)
        query_block = query_all[inner_step].reshape(query_rows, local_groups, KVH, HD)
        cotangent_block = cotangent_all[inner_step].reshape(query_rows, local_groups, KVH, HD)
        block_part = block_gradient(key_values, query_block, cotangent_block, first_row)
        key_value_grad = lax.psum(block_part.astype(jnp.bfloat16), ("fsdp", "tp"))
        update = jnp.dot(features, key_value_grad, preferred_element_type=jnp.float32)
        inner = inner - INNER_RATE * (update * scale)
    weight_delta = (weights_low.astype(jnp.float32) - inner).astype(jnp.bfloat16)
    stacked = partner_value(
        jnp.stack([weights_low, weight_delta]),
        mask_value,
        bit_count,
        lambda payload, bit_index: from_partner(payload, "rep", bit_index),
    )
    partner_weights = stacked[0]
    partner_delta = stacked[1]
    outer_full = weights_low.astype(jnp.float32)
    step_change = (
        MOMENTUM_DECAY * momentum_low.astype(jnp.float32)
        - DELTA_WEIGHT * (weight_delta.astype(jnp.float32) + partner_delta.astype(jnp.float32))
        - PAIR_WEIGHT * (outer_full - partner_weights.astype(jnp.float32))
    )
    return (
        (outer_full + step_change).astype(jnp.bfloat16)[None],
        step_change.astype(jnp.bfloat16)[None],
    )


def solution(mesh):
    in_specs = (
        P("rep", None, ("fsdp", "tp"), None),
        P("rep", None, "fsdp", "tp"),
        P("rep", None, "fsdp", "tp"),
        P("rep", ("fsdp", "tp"), None),
        P("rep", ("fsdp", "tp"), None),
        P(),
    )
    out_specs = (P("rep", ("fsdp", "tp"), None), P("rep", ("fsdp", "tp"), None))
    return jax.shard_map(
        on_device, mesh=mesh, in_specs=in_specs, out_specs=out_specs, check_vma=False
    )
```

profile of v0, /device:TPU:99, one launch (start us, length us, event | category | flops | bytes accessed | tf_op | source)
XLA Modules:
  0.0 885.8 jit_solution(11521131750914079580)
XLA Ops:
  7.2 3.0 convolution_convert_fusion.1
  10.4 0.4 reshape.149
  10.8 0.4 multiply_reduce_fusion.5
  11.3 0.1 copy.69
  11.5 0.7 fusion.79
  12.3 0.9 reshape_squeeze.8
  13.1 0.7 iota_compare_fusion
  13.8 1.0 multiply_convert_fusion.7
  14.9 115.6 %all-reduce.5.cloned.1.call-done = bf16[512,1024]{1,0:T(8,128)(2,1)} async-done(((bf16[512,1024]{1,0:T(8,128)(2,1)}), bf16[512,1024]{1,0:T(8,128)(2,1)}) %all-reduce.5.cloned.1.call-update) | async-done | bytes 1048592 | tf_op jit(solution)/shard_map/psum | solution.py:105
  130.5 1.5 multiply_convert_fusion.1
  132.1 0.4 reshape.151
  132.5 0.4 copy.71
  132.9 0.6 multiply_reduce_fusion.3
  133.8 2.7 fusion.47
  136.5 0.7 fusion.9
  137.2 1.3 copy-done.3
  138.5 1.5 fusion.28
  140.0 9.4 %multiply_reduce_fusion.2 = (f32[512,4]{0,1:T(4,128)S(1)}, f32[512,4,128]{0,2,1:T(8,128)S(1)}) fusion(f32[512,4,128]{0,2,1:T(8,128)S(1)} %copy.71, f32[512,4]{0,1:T(4,128)S(1)} %add_rsqrt_fusion.2, f32[4,512,64,4]{1,2,3,0:T(8,128)} %fusion.47, f32[4,4,64]{2,1,0:T(4,128)S(1)} %get-tuple-element.12, f32[4,512,64,4]{1,2,3,0:T(8,128)} %copy-done.3, ...), kind=kOutput, calls=%fused_computation.63 | convolution fusion | flops 140770816 | bytes 6606848 | tf_op jit(solution)/shard_map/kgrs,rgkd->skd/dot_general | solution.py:65
  149.4 0.3 multiply_convert_fusion.3
  149.7 0.7 copy-done.16
  150.5 1.1 pad_maximum_fusion.1
  151.6 117.2 %all-reduce.7.cloned.1.call-done = bf16[512,1024]{0,1:T(8,128)(2,1)} async-done(((bf16[512,1024]{0,1:T(8,128)(2,1)}), bf16[512,1024]{0,1:T(8,128)(2,1)}) %all-reduce.7.cloned.1.call-update) | async-done | bytes 1048592 | tf_op jit(solution)/shard_map/psum | solution.py:110
  268.8 1.8 convert_subtract_fusion.2
  270.6 1.8 fusion.19
  272.4 0.2 all-reduce.11.cloned.1.call-start
  272.6 0.4 reshape.152
  273.0 0.4 multiply_reduce_fusion.4
  273.6 0.1 copy.79
  273.7 0.9 reshape_squeeze.9
  274.6 1.0 multiply_convert_fusion.6
  275.6 114.0 %all-reduce.9.cloned.1.call-done = bf16[512,1024]{1,0:T(8,128)(2,1)} async-done(((bf16[512,1024]{1,0:T(8,128)(2,1)}), bf16[512,1024]{1,0:T(8,128)(2,1)}) %all-reduce.9.cloned.1.call-update) | async-done | bytes 1048592 | tf_op jit(solution)/shard_map/psum | solution.py:105
  389.7 1.5 multiply_convert_fusion
  391.1 1.1 fusion.77
  392.2 1.6 reshape.154
  393.8 1.4 copy.82
  395.2 1.3 multiply_reduce_fusion.1
  396.5 1.7 copy.81
  398.2 0.7 add_rsqrt_fusion
  398.9 0.9 reshape.146
  399.9 2.9 fusion.45
  402.8 0.7 fusion.11
  403.5 1.3 copy-done.2
  404.8 1.5 fusion.29
  406.3 10.4 %multiply_reduce_fusion = (f32[512,4]{0,1:T(4,128)S(1)}, f32[512,4,128]{0,2,1:T(8,128)}) fusion(f32[512,4,128]{0,2,1:T(8,128)S(1)} %copy-done.1, f32[512,4]{0,1:T(4,128)S(1)} %add_rsqrt_fusion, f32[4,512,64,4]{1,2,3,0:T(8,128)} %fusion.45, f32[4,4,64]{2,1,0:T(4,128)} %copy-done.20, f32[4,512,64,4]{1,2,3,0:T(8,128)} %copy-done.2, ...), kind=kOutput, calls=%fused_computation.59 | convolution fusion | flops 140770816 | bytes 6606848 | tf_op jit(solution)/shard_map/kgrs,rgkd->skd/dot_general | solution.py:65
  416.7 1.6 multiply_convert_fusion.2
  418.3 1.1 pad_maximum_fusion.2
  419.4 117.3 %all-reduce.11.cloned.1.call-done = bf16[512,1024]{0,1:T(8,128)(2,1)} async-done(((bf16[512,1024]{0,1:T(8,128)(2,1)}), bf16[512,1024]{0,1:T(8,128)(2,1)}) %all-reduce.11.cloned.1.call-update) | async-done | bytes 1048592 | tf_op jit(solution)/shard_map/psum | solution.py:110
  536.7 1.8 fusion.22
  538.7 4.1 collective-permute-start
  543.4 2.0 collective-permute-done
  545.4 0.2 broadcast_select_fusion
  545.6 2.1 collective-permute-start.1
  547.7 29.8 %collective-permute-done.1 = bf16[2,320,1024]{2,1,0:T(8,128)(2,1)S(1)} collective-permute-done((bf16[2,320,1024]{2,1,0:T(8,128)(2,1)S(1)}, bf16[2,320,1024]{2,1,0:T(8,128)(2,1)S(1)}, u32[]{:S(2)}, u32[]{:S(2)}) %collective-permute-start.1) | collective-permute-done | bytes 1310752 | tf_op jit(solution)/shard_map/ppermute | solution.py:23
  577.5 0.3 broadcast_select_fusion.1
  577.7 2.0 collective-permute-start.2
  579.7 59.5 %collective-permute-done.2 = bf16[2,320,1024]{2,1,0:T(8,128)(2,1)S(1)} collective-permute-done((bf16[2,320,1024]{2,1,0:T(8,128)(2,1)S(1)}, bf16[2,320,1024]{2,1,0:T(8,128)(2,1)S(1)}, u32[]{:S(2)}, u32[]{:S(2)}) %collective-permute-start.2) | collective-permute-done | bytes 1310752 | tf_op jit(solution)/shard_map/ppermute | solution.py:23
  639.2 0.1 broadcast_select_fusion.2
  639.3 7.4 collective-permute-start.3
  646.7 137.2 %collective-permute-done.3 = bf16[2,320,1024]{2,1,0:T(8,128)(2,1)S(1)} collective-permute-done((bf16[2,320,1024]{2,1,0:T(8,128)(2,1)S(1)}, bf16[2,320,1024]{2,1,0:T(8,128)(2,1)S(1)}, u32[]{:S(2)}, u32[]{:S(2)}) %collective-permute-start.3) | collective-permute-done | bytes 1310752 | tf_op jit(solution)/shard_map/ppermute | solution.py:23
  783.9 0.2 broadcast_select_fusion.3
  784.1 7.3 collective-permute-start.4
  791.5 85.8 %collective-permute-done.4 = bf16[2,320,1024]{2,1,0:T(8,128)(2,1)S(1)} collective-permute-done((bf16[2,320,1024]{2,1,0:T(8,128)(2,1)S(1)}, bf16[2,320,1024]{2,1,0:T(8,128)(2,1)S(1)}, u32[]{:S(2)}, u32[]{:S(2)}) %collective-permute-start.4) | collective-permute-done | bytes 1310752 | tf_op jit(solution)/shard_map/ppermute | solution.py:23
  877.2 0.2 broadcast_select_fusion.4
  877.4 1.8 convert_bitcast_fusion
  (59 shorter events, 1.1 us)
Async XLA Ops:
  7.2 3.1 copy-start.13
  7.2 123.3 %all-reduce.5.cloned.1.call-start = ((), (), s32[]{:S(2)}) async-start(), calls=%async_computation | async-start | bytes 2097152 | tf_op jit(solution)/shard_map/psum | solution.py:105
  10.2 1.3 copy-start.14
  10.2 258.6 %all-reduce.7.cloned.1.call-start = ((), (), s32[]{:S(2)}) async-start(), calls=%async_computation.1 | async-start | bytes 2097152 | tf_op jit(solution)/shard_map/psum | solution.py:110
  10.4 120.1 %copy-start.19 = (f32[1024]{0:T(1024)S(1)}, f32[1024]{0:T(1024)}, u32[]{:S(2)}) copy-start(f32[1024]{0:T(1024)} %constant.50.clone.1) | copy-start | bytes 12292
  133.5 3.0 copy-start.8
  133.5 3.0 copy-start.17
  136.5 2.0 copy-start.10
  137.2 1.3 copy-start.3
  138.5 1.5 copy-start.9
  149.4 1.0 copy-start.16
  149.7 119.1 %copy-start = (bf16[1,320,1024]{2,1,0:T(8,128)(2,1)S(1)}, bf16[1,320,1024]{2,1,0:T(8,128)(2,1)}, u32[]{:S(2)}) copy-start(bf16[1,320,1024]{2,1,0:T(8,128)(2,1)} %param.9) | copy-start | bytes 1966084
  149.7 119.1 %copy-start.4 = (bf16[1,2,320,512]{3,2,1,0:T(8,128)(2,1)S(1)}, bf16[1,2,320,512]{3,2,1,0:T(8,128)(2,1)}, u32[]{:S(2)}) copy-start(bf16[1,2,320,512]{3,2,1,0:T(8,128)(2,1)} %param.6) | copy-start | bytes 1966084
  151.6 238.1 %all-reduce.9.cloned.1.call-start = ((), (), s32[]{:S(2)}) async-start(), calls=%async_computation.2 | async-start | bytes 2097152 | tf_op jit(solution)/shard_map/psum | solution.py:105
  272.4 1.3 copy-start.6
  272.4 264.3 %all-reduce.11.cloned.1.call-start = ((), (), s32[]{:S(2)}) async-start(), calls=%async_computation.3 | async-start | bytes 2097152 | tf_op jit(solution)/shard_map/psum | solution.py:110
  396.5 6.3 copy-start.1
  399.9 2.9 copy-start.7
  399.9 2.9 copy-start.18
  402.8 2.0 copy-start.11
  403.5 1.3 copy-start.2
  403.5 1.3 copy-start.20
  416.7 1.6 copy-start.15
  418.3 118.4 %copy-start.5 = (bf16[1,2,320,512]{3,2,1,0:T(8,128)(2,1)S(1)}, bf16[1,2,320,512]{3,2,1,0:T(8,128)(2,1)}, u32[]{:S(2)}) copy-start(bf16[1,2,320,512]{3,2,1,0:T(8,128)(2,1)} %param.6) | copy-start | bytes 1966084
  538.7 6.7 collective-permute-start
  545.6 31.9 %collective-permute-start.1 = (bf16[2,320,1024]{2,1,0:T(8,128)(2,1)S(1)}, bf16[2,320,1024]{2,1,0:T(8,128)(2,1)S(1)}, u32[]{:S(2)}, u32[]{:S(2)}) collective-permute-start(bf16[2,320,1024]{2,1,0:T(8,128)(2,1)S(1)} %broadcast_select_fusion), channel_id=1, source_target_pairs={{0,32},{16,48},{32,0},{48,16},{64,96},{80,112},{96,64},{112,80},{1... | collective-permute-start | bytes 3932168 | tf_op jit(solution)/shard_map/ppermute | solution.py:23
  577.7 61.5 %collective-permute-start.2 = (bf16[2,320,1024]{2,1,0:T(8,128)(2,1)S(1)}, bf16[2,320,1024]{2,1,0:T(8,128)(2,1)S(1)}, u32[]{:S(2)}, u32[]{:S(2)}) collective-permute-start(bf16[2,320,1024]{2,1,0:T(8,128)(2,1)S(1)} %broadcast_select_fusion.1), channel_id=1, source_target_pairs={{0,64},{16,80},{32,96},{48,112},{64,0},{80,16},{96,32},{112,48},{1... | collective-permute-start | bytes 3932168 | tf_op jit(solution)/shard_map/ppermute | solution.py:23
  639.3 144.6 %collective-permute-start.3 = (bf16[2,320,1024]{2,1,0:T(8,128)(2,1)S(1)}, bf16[2,320,1024]{2,1,0:T(8,128)(2,1)S(1)}, u32[]{:S(2)}, u32[]{:S(2)}) collective-permute-start(bf16[2,320,1024]{2,1,0:T(8,128)(2,1)S(1)} %broadcast_select_fusion.2), channel_id=1, source_target_pairs={{0,128},{16,144},{32,160},{48,176},{64,192},{80,208},{96,224},{112... | collective-permute-start | bytes 3932168 | tf_op jit(solution)/shard_map/ppermute | solution.py:23
  784.1 93.3 %copy-start.12 = (bf16[1,320,1024]{2,1,0:T(8,128)(2,1)S(1)}, bf16[1,320,1024]{2,1,0:T(8,128)(2,1)}, u32[]{:S(2)}) copy-start(bf16[1,320,1024]{2,1,0:T(8,128)(2,1)} %param.10) | copy-start | bytes 1966084
  784.1 93.1 %collective-permute-start.4 = (bf16[2,320,1024]{2,1,0:T(8,128)(2,1)S(1)}, bf16[2,320,1024]{2,1,0:T(8,128)(2,1)S(1)}, u32[]{:S(2)}, u32[]{:S(2)}) collective-permute-start(bf16[2,320,1024]{2,1,0:T(8,128)(2,1)S(1)} %broadcast_select_fusion.3), channel_id=1, source_target_pairs={{0,256},{16,272},{32,288},{48,304},{64,320},{80,336},{96,352},{112... | collective-permute-start | bytes 3932168 | tf_op jit(solution)/shard_map/ppermute | solution.py:23
Sparse Core Ops, SparseCore 0:
  11.3 119.2 all-reduce.4
  151.7 117.0 all-reduce.6
  272.5 117.0 all-reduce.8
  419.5 117.1 all-reduce.10
where the time goes:
time: 887 us; the launch traced here: 886 us
  waiting for transfers between devices  778 us (88%)
  matrix products  38.2 us (4%)
  starting transfers between devices  23.2 us (3%)
  other arithmetic  17.5 us (2%)
  between operations  14.8 us (2%)
  local copies, waits for them, and re-layouts  13.6 us (2%)
    ppermute x5, waiting for transfers between devices, from_partner(): return lax.ppermute(value, axis, pairs)  314 us
    psum x2, waiting for transfers between devices, on_device(): key_value_grad = lax.psum(block_part.astype(jnp.bfloat16), ('fsdp', 'tp'))  234 us
    psum x2, waiting for transfers between devices, on_device(): lax.psum(partial_value.astype(jnp.bfloat16), ('fsdp', 'tp'))  230 us
    ppermute x5, starting transfers between devices, from_partner(): return lax.ppermute(value, axis, pairs)  22.9 us
    dot_general x2, matrix products, block_gradient(): jnp.einsum('kgrs,rgkd->skd', score_low, query_low, preferred_element_type...  19.8 us
  transfers between devices with their start and end apart: 9, of which 9 were waited for; matrix products, arithmetic and copies ran while one was open for 1% of the time, Pallas kernels for 0%

commit v1 on v0

v1 whole, which is shorter than its diff:
```python
import functools

import jax
import jax.numpy as jnp
from jax import lax
from jax.experimental import pallas as pl
from jax.experimental.pallas import tpu as pltpu
from jax.sharding import PartitionSpec as P

D = 5120
HD = 128
KVH = 4
GROUP = 8
STEPS = 2

EPSILON = 1e-06
INNER_RATE = 8.0
MOMENTUM_DECAY = 0.9
DELTA_WEIGHT = 0.35
PAIR_WEIGHT = 0.25

MESH = pl.DeviceIdType.MESH
HOPS = 4
SKEW = 2
CHUNK = 128
VALUE_SCALE = D ** (-0.5)
HEAD_SCALE = HD ** (-0.5)


def neighbour_ids():
    rep, f, t = lax.axis_index("rep"), lax.axis_index("fsdp"), lax.axis_index("tp")
    x_lo, y = f % 2, f // 2
    y_lo, y_hi = y % 2, y // 2
    flip_x = f + 1 - 2 * x_lo
    flip_y_lo = f + 2 - 4 * y_lo
    ids = [
        (rep, flip_x, t),
        (rep, flip_x, 1 - t),
        (rep, flip_y_lo, t),
        (rep, 2 * (3 - y) + x_lo, t),
    ]
    bits = [(x_lo + t) % 2, t, (y_lo + y_hi) % 2, y_hi]
    return ids, bits


def front_kernel(
    tok_ref,
    query_ref,
    cot_in_ref,
    w_ref,
    payload_ref,
    delta_ref,
    theta,
    acc,
    gathered,
    landed,
    staged,
    query_low,
    cot,
    rs_send,
    rs_recv,
    ag_send,
    ag_recv,
):
    seq = tok_ref.shape[2]
    query_rows = query_ref.shape[1]
    groups = query_ref.shape[2] // (KVH * HD)
    lanes = groups * query_rows
    ids, bits = neighbour_ids()
    first_row = lax.axis_index("fsdp") * query_rows

    barrier = pltpu.get_barrier_semaphore()
    for other in ids:
        pl.semaphore_signal(barrier, inc=1, device_id=other, device_id_type=MESH)

    size = [seq >> (k + 1) for k in range(HOPS)]
    offset = [sum(size[:k]) for k in range(HOPS)]

    def dim(h, k):
        return (h + k) % HOPS

    base = []
    for h in range(KVH):
        starts = [jnp.int32(0)]
        for k in range(HOPS):
            starts.append(starts[-1] + bits[dim(h, k)] * size[k])
        base.append(starts)

    def rows(start, count):
        return pl.ds(pl.multiple_of(start, size[HOPS - 1]), count)

    def rs_copy(ar, h, k):
        part = (ar * KVH + h, pl.ds(offset[k], size[k]))
        return pltpu.make_async_remote_copy(
            src_ref=staged.at[part],
            dst_ref=landed.at[part],
            send_sem=rs_send.at[h, k],
            recv_sem=rs_recv.at[h, k],
            device_id=ids[dim(h, k)],
            device_id_type=MESH,
        )

    def ag_copy(ar, h, k):
        back = HOPS - 1 - k
        part = (ar * KVH + h, rows(base[h][back + 1], size[back]))
        return pltpu.make_async_remote_copy(
            src_ref=gathered.at[part],
            dst_ref=gathered.at[part],
            send_sem=ag_send.at[h, k],
            recv_sem=ag_recv.at[h, k],
            device_id=ids[dim(h, back)],
            device_id_type=MESH,
        )

    def begin_sum(ar, h):
        bit = bits[dim(h, 0)]
        n = size[0]
        staged[ar * KVH + h, pl.ds(offset[0], n)] = acc[h, rows((1 - bit) * n, n)].astype(jnp.bfloat16)
        rs_copy(ar, h, 0).start()

    def halve(ar, h, k):
        rs_copy(ar, h, k).wait()
        slot = ar * KVH + h
        start = base[h][k + 1]
        if k < HOPS - 1:
            n = size[k + 1]
            bit = bits[dim(h, k + 1)]
            gone, kept = (1 - bit) * n, bit * n
            total = acc[h, rows(start + gone, n)] + landed[slot, rows(offset[k] + gone, n)].astype(jnp.float32)
            staged[slot, pl.ds(offset[k + 1], n)] = total.astype(jnp.bfloat16)
            rs_copy(ar, h, k + 1).start()
            acc[h, rows(start + kept, n)] = acc[h, rows(start + kept, n)] + landed[
                slot, rows(offset[k] + kept, n)
            ].astype(jnp.float32)
        else:
            n = size[k]
            total = acc[h, rows(start, n)] + landed[slot, pl.ds(offset[k], n)].astype(jnp.float32)
            if ar % 2 == 0:
                total = jnp.concatenate([total[:, :HD], total[:, HD:] * VALUE_SCALE], axis=1)
            gathered[slot, rows(start, n)] = total.astype(jnp.bfloat16)
            ag_copy(ar, h, 0).start()

    def widen(ar, h, k):
        ag_copy(ar, h, k).wait()
        if k < HOPS - 1:
            ag_copy(ar, h, k + 1).start()

    def key_cols(h):
        return pl.ds(h * HD, HD)

    def value_cols(h):
        return pl.ds(KVH * HD + h * HD, HD)

    def project(s, h, low):
        acc[h] = lax.dot_general(
            tok_ref[s], low, (((0,), (0,)), ((), ())), preferred_element_type=jnp.float32
        )

    def prepare(s, h):
        for g in range(groups):
            cols = pl.ds((g * KVH + h) * HD, HD)
            q = query_ref[s, :, cols].astype(jnp.float32)
            norm = lax.rsqrt(jnp.mean(q * q, axis=-1, keepdims=True) + EPSILON)
            query_low[s, h, pl.ds(g * query_rows, query_rows)] = (q * norm).astype(jnp.bfloat16)
            cot[s, h, pl.ds(g * query_rows, query_rows)] = cot_in_ref[s, :, cols]

    def attend(s, h):
        slot = 2 * s * KVH + h
        q = query_low[s, h]
        c = cot[s, h]
        contract_last = (((1,), (1,)), ((), ()))
        position = first_row + lax.broadcasted_iota(jnp.int32, (CHUNK, lanes), 1) % query_rows
        row = lax.broadcasted_iota(jnp.int32, (CHUNK, lanes), 0)
        raised, prob_grad = [], []
        denom = jnp.zeros((1, lanes), jnp.float32)
        mixed = jnp.zeros((1, lanes), jnp.float32)
        units, norms = [], []
        for i in range(seq // CHUNK):
            part = pl.ds(i * CHUNK, CHUNK)
            keys = gathered[slot, part, :HD].astype(jnp.float32)
            norm = lax.rsqrt(jnp.mean(keys * keys, axis=-1, keepdims=True) + EPSILON)
            unit = keys * norm
            units.append(unit)
            norms.append(norm)
            scores = lax.dot_general(
                unit.astype(jnp.bfloat16), q, contract_last, preferred_element_type=jnp.float32
            )
            e = jnp.where(row + i * CHUNK <= position, jnp.exp(scores * HEAD_SCALE), 0.0)
            pg = lax.dot_general(
                gathered[slot, part, HD:], c, contract_last, preferred_element_type=jnp.float32
            )
            denom = denom + jnp.sum(e, axis=0, keepdims=True)
            mixed = mixed + jnp.sum(e * pg, axis=0, keepdims=True)
            raised.append(e)
            prob_grad.append(pg)
        inverse = 1.0 / denom
        mixed = mixed * inverse
        for i in range(seq // CHUNK):
            part = pl.ds(i * CHUNK, CHUNK)
            probs = raised[i] * inverse
            score_low = (probs * (prob_grad[i] - mixed) * HEAD_SCALE).astype(jnp.bfloat16)
            acc[h, part, HD:] = jnp.dot(probs.astype(jnp.bfloat16), c, preferred_element_type=jnp.float32)
            unit_grad = jnp.dot(score_low, q, preferred_element_type=jnp.float32)
            unit = units[i]
            acc[h, part, :HD] = (
                unit_grad - unit * jnp.mean(unit_grad * unit, axis=-1, keepdims=True)
            ) * norms[i]

    def descend(s, h):
        slot = (2 * s + 1) * KVH + h
        update = jnp.dot(tok_ref[s], gathered[slot], preferred_element_type=jnp.float32)
        scale = jnp.where(
            lax.broadcasted_iota(jnp.int32, (1, 2 * HD), 1) < HD, INNER_RATE, INNER_RATE * VALUE_SCALE
        )
        return theta[h] - update * scale

    def weights(h):
        return jnp.concatenate([w_ref[:, key_cols(h)], w_ref[:, value_cols(h)]], axis=1)

    def finish(h):
        low = weights(h).astype(jnp.float32)
        delta = (low - descend(STEPS - 1, h)).astype(jnp.bfloat16)
        payload = (PAIR_WEIGHT * low - DELTA_WEIGHT * delta.astype(jnp.float32)).astype(jnp.bfloat16)
        delta_ref[:, key_cols(h)] = delta[:, :HD]
        delta_ref[:, value_cols(h)] = delta[:, HD:]
        payload_ref[:, key_cols(h)] = payload[:, :HD]
        payload_ref[:, value_cols(h)] = payload[:, HD:]

    def task(h, index):
        ar, stage = index // (2 * HOPS), index % (2 * HOPS)
        if stage == 0:
            if ar > 0:
                widen(ar - 1, h, HOPS - 1)
            s = ar // 2
            if ar == 2 * STEPS:
                finish(h)
                return
            if ar % 2 == 1:
                attend(s, h)
            elif s == 0:
                low = weights(h)
                theta[h] = low.astype(jnp.float32)
                project(0, h, low)
            else:
                new = descend(s - 1, h)
                theta[h] = new
                project(s, h, new.astype(jnp.bfloat16))
            if ar == 0 and h == 0:
                pl.semaphore_wait(barrier, len(ids))
            begin_sum(ar, h)
            if ar % 2 == 0:
                prepare(s, h)
        elif stage <= HOPS:
            halve(ar, h, stage - 1)
        else:
            widen(ar, h, stage - HOPS - 1)

    last = 4 * HOPS * STEPS
    for tick in range(last + SKEW * (KVH - 1) + 1):
        for h in range(KVH):
            index = tick - SKEW * h
            if 0 <= index <= last:
                task(h, index)


def front(tokens, queries, cotangent, weights_low):
    steps, features, seq = tokens.shape
    columns = weights_low.shape[1]
    lanes = queries.shape[2] // (KVH * HD) * queries.shape[1]
    sums = 2 * steps * KVH
    vmem = pl.BlockSpec(memory_space=pltpu.VMEM)
    out = jax.ShapeDtypeStruct((features, columns), jnp.bfloat16)
    return pl.pallas_call(
        front_kernel,
        out_shape=(out, out),
        in_specs=[vmem] * 4,
        out_specs=(vmem, vmem),
        scratch_shapes=[
            pltpu.VMEM((KVH, features, 2 * HD), jnp.float32),
            pltpu.VMEM((KVH, seq, 2 * HD), jnp.float32),
            pltpu.VMEM((sums, seq, 2 * HD), jnp.bfloat16),
            pltpu.VMEM((sums, seq, 2 * HD), jnp.bfloat16),
            pltpu.VMEM((sums, seq, 2 * HD), jnp.bfloat16),
            pltpu.VMEM((steps, KVH, lanes, HD), jnp.bfloat16),
            pltpu.VMEM((steps, KVH, lanes, HD), jnp.bfloat16),
            pltpu.SemaphoreType.DMA((KVH, HOPS)),
            pltpu.SemaphoreType.DMA((KVH, HOPS)),
            pltpu.SemaphoreType.DMA((KVH, HOPS)),
            pltpu.SemaphoreType.DMA((KVH, HOPS)),
        ],
        compiler_params=pltpu.CompilerParams(
            collective_id=0, has_side_effects=True, vmem_limit_bytes=40 * 1024 * 1024
        ),
    )(tokens, queries, cotangent, weights_low)


def from_partner(value, mask_value):
    replicas = lax.axis_size("rep")

    def by(mask, value):
        return lax.ppermute(value, "rep", [(source, source ^ mask) for source in range(replicas)])

    return lax.switch(mask_value - 1, [functools.partial(by, mask) for mask in range(1, replicas)], value)


def on_device(tokens, queries, cotangent, outer_weights, momentum, partner_mask):
    weights_low = outer_weights[0]
    momentum_low = momentum[0]
    payload, weight_delta = front(tokens[0], queries[0], cotangent[0], weights_low)
    partner_payload = from_partner(payload, partner_mask[0])
    outer_full = weights_low.astype(jnp.float32)
    step_change = (
        MOMENTUM_DECAY * momentum_low.astype(jnp.float32)
        - DELTA_WEIGHT * weight_delta.astype(jnp.float32)
        - PAIR_WEIGHT * outer_full
        + partner_payload.astype(jnp.float32)
    )
    return (
        (outer_full + step_change).astype(jnp.bfloat16)[None],
        step_change.astype(jnp.bfloat16)[None],
    )


def solution(mesh):
    in_specs = (
        P("rep", None, ("fsdp", "tp"), None),
        P("rep", None, "fsdp", "tp"),
        P("rep", None, "fsdp", "tp"),
        P("rep", ("fsdp", "tp"), None),
        P("rep", ("fsdp", "tp"), None),
        P(),
    )
    out_specs = (P("rep", ("fsdp", "tp"), None), P("rep", ("fsdp", "tp"), None))
    return jax.shard_map(
        on_device, mesh=mesh, in_specs=in_specs, out_specs=out_specs, check_vma=False
    )
```

time: 887 us -> 227 us (0.26)
  the two profiles are of different devices: /device:TPU:99 before, /device:TPU:1 now
where the time goes in v1:
time: 227 us
  Pallas kernels  151 us (67%)
  waiting for transfers between devices  57 us (25%)
  starting transfers between devices  10.4 us (5%)
  local copies, waits for them, and re-layouts  4.26 us (2%)
  other arithmetic  2.76 us (1%)
    pallas_call x1, Pallas kernels, front(): pl.pallas_call(front_kernel, out_shape=(out, out), in_specs=[vmem] * 4, o...  151 us
    ppermute x1, waiting for transfers between devices, by(): lax.ppermute(value, 'rep', [(source, source ^ mask) for source in range(r...  57 us
    ppermute x1, starting transfers between devices, by(): lax.ppermute(value, 'rep', [(source, source ^ mask) for source in range(r...  10.4 us
  transfers between devices with their start and end apart: 1, of which 1 were waited for; matrix products, arithmetic and copies ran while one was open for 0% of the time, Pallas kernels for 0%

profile of v1, /device:TPU:1, one launch (start us, length us, event | category | flops | bytes accessed | tf_op | source)
XLA Modules:
  0.0 226.7 jit_solution(1292900939790598602)
XLA Ops:
  1.3 0.0 copy-start
  1.3 1.1 copy-done
  2.4 0.0 copy-start.2
  2.4 1.1 copy-done.2
  3.5 0.0 copy-start.3
  3.5 1.0 copy-done.3
  4.5 0.0 copy-start.4
  4.5 1.0 copy-done.4
  5.5 0.0 copy-start.1
  5.5 0.0 copy-start.5
  5.5 151.0 %shard_map.77 = (bf16[320,1024]{1,0:T(8,128)(2,1)S(1)}, bf16[320,1024]{1,0:T(8,128)(2,1)S(1)}) custom-call(bf16[2,320,512]{2,1,0:T(8,128)(2,1)S(1)} %bitcast.20, bf16[2,64,2048]{2,1,0:T(8,128)(2,1)S(1)} %bitcast.21, bf16[2,64,2048]{2,1,0:T(8,128)(2,1)S(1)} %bitcast.22, bf16[320,1024]{1,0:T(8,128)(2,1)S(1)} %bitcast.19), custom_call_target="tpu_custom_call" | custom-call | tf_op jit(solution)/shard_map/pallas_call | solution.py:273
  156.5 67.4 %conditional.4 = (bf16[320,1024]{1,0:T(8,128)(2,1)}) conditional(s32[]{:T(128)} %bitcast.5, bf16[320,1024]{1,0:T(8,128)(2,1)S(1)} %get-tuple-element.74, bf16[320,1024]{1,0:T(8,128)(2,1)S(1)} %get-tuple-element.74, bf16[320,1024]{1,0:T(8,128)(2,1)S(1)} %get-tuple-element.74, ...), branch_computations={%region_0.0_spmd, %region_1.0_spmd, %region_2.0_spmd, %region_3.0_... | conditional | bytes 2621488
  156.6 10.4 %collective-permute-start.29 = (bf16[320,1024]{1,0:T(8,128)(2,1)S(1)}, bf16[320,1024]{1,0:T(8,128)(2,1)}, u32[]{:S(2)}, u32[]{:S(2)}) collective-permute-start(bf16[320,1024]{1,0:T(8,128)(2,1)S(1)} %param.29), channel_id=1, source_target_pairs={{0,480},{16,496},{32,448},{48,464},{64,416},{80,432},{96,384},{112... | collective-permute-start | bytes 1966088 | tf_op jit(solution)/shard_map/cond/branch_29_fun/ppermute | solution.py:301
  167.0 57.0 %collective-permute-done.29 = bf16[320,1024]{1,0:T(8,128)(2,1)} collective-permute-done((bf16[320,1024]{1,0:T(8,128)(2,1)S(1)}, bf16[320,1024]{1,0:T(8,128)(2,1)}, u32[]{:S(2)}, u32[]{:S(2)}) %collective-permute-start.29) | collective-permute-done | bytes 655392 | tf_op jit(solution)/shard_map/cond/branch_29_fun/ppermute | solution.py:301
  224.0 0.0 copy-done.1
  224.0 0.0 copy-done.5
  224.0 2.8 %convert_bitcast_fusion = (bf16[1,320,1024]{2,1,0:T(8,128)(2,1)}, bf16[1,320,1024]{2,1,0:T(8,128)(2,1)}) fusion(bf16[320,1024]{1,0:T(8,128)(2,1)} %get-tuple-element.77, bf16[320,1024]{1,0:T(8,128)(2,1)S(1)} %get-tuple-element.73, bf16[1,320,1024]{2,1,0:T(8,128)(2,1)S(1)} %copy-done.5, bf16[1,320,1024]{2,1,0:T(8,128)(2,1)S(1)} %copy-done.1), kind=kLoop, calls=%fused_computation.7 | loop fusion | flops 4259840 | bytes 3932160 | tf_op jit(solution)/shard_map/broadcast_in_dim | solution.py:320
Async XLA Ops:
  1.3 1.1 copy-start
  2.4 1.1 copy-start.2
  3.5 1.0 copy-start.3
  4.5 1.0 copy-start.4
  5.5 218.4 %copy-start.1 = (bf16[1,320,1024]{2,1,0:T(8,128)(2,1)S(1)}, bf16[1,320,1024]{2,1,0:T(8,128)(2,1)}, u32[]{:S(2)}) copy-start(bf16[1,320,1024]{2,1,0:T(8,128)(2,1)} %param.40) | copy-start | bytes 1966084
  5.5 218.4 %copy-start.5 = (bf16[1,320,1024]{2,1,0:T(8,128)(2,1)S(1)}, bf16[1,320,1024]{2,1,0:T(8,128)(2,1)}, u32[]{:S(2)}) copy-start(bf16[1,320,1024]{2,1,0:T(8,128)(2,1)} %param.41) | copy-start | bytes 1966084
  156.6 67.4 %collective-permute-start.29 = (bf16[320,1024]{1,0:T(8,128)(2,1)S(1)}, bf16[320,1024]{1,0:T(8,128)(2,1)}, u32[]{:S(2)}, u32[]{:S(2)}) collective-permute-start(bf16[320,1024]{1,0:T(8,128)(2,1)S(1)} %param.29), channel_id=1, source_target_pairs={{0,480},{16,496},{32,448},{48,464},{64,416},{80,432},{96,384},{112... | collective-permute-start | bytes 1966088 | tf_op jit(solution)/shard_map/cond/branch_29_fun/ppermute | solution.py:301

commit v2 on v1

v2 whole, which is shorter than its diff:
```python
import functools

import jax
import jax.numpy as jnp
from jax import lax
from jax.experimental import pallas as pl
from jax.experimental.pallas import tpu as pltpu
from jax.sharding import PartitionSpec as P

D = 5120
HD = 128
KVH = 4
GROUP = 8
STEPS = 2

EPSILON = 1e-06
INNER_RATE = 8.0
MOMENTUM_DECAY = 0.9
DELTA_WEIGHT = 0.35
PAIR_WEIGHT = 0.25

MESH = pl.DeviceIdType.MESH
RING = 4
SKEW = 0
VALUE_SCALE = D ** (-0.5)
HEAD_SCALE = HD ** (-0.5)


def ring_ids(axis):
    rep, f, t = lax.axis_index("rep"), lax.axis_index("fsdp"), lax.axis_index("tp")
    x, y = t * 2 + f % 2, f // 2
    if axis == 0:
        others = [(x + r) % RING for r in range(1, RING)]
        return x, [(rep, y * 2 + other % 2, other // 2) for other in others]
    others = [(y + r) % RING for r in range(1, RING)]
    return y, [(rep, other * 2 + f % 2, t) for other in others]


def front_kernel(
    tok_ref,
    query_ref,
    cot_in_ref,
    w_ref,
    payload_ref,
    delta_ref,
    theta,
    gathered,
    staged,
    landed,
    partial,
    crossed,
    query_low,
    cot,
    raised,
    prob_grad,
    units,
    norms,
    send_sem,
    recv_sem,
):
    seq = tok_ref.shape[2]
    query_rows = query_ref.shape[1]
    groups = query_ref.shape[2] // (KVH * HD)
    lanes = groups * query_rows
    block = seq // RING
    piece = block // RING
    rings = [ring_ids(0), ring_ids(1)]
    first_row = lax.axis_index("fsdp") * query_rows

    barrier = pltpu.get_barrier_semaphore()
    for _, ids in rings:
        for other in ids:
            pl.semaphore_signal(barrier, inc=1, device_id=other, device_id_type=MESH)

    def ring(h, phase):
        return rings[(h + phase) % 2]

    def rows(start, count):
        return pl.ds(pl.multiple_of(start, piece), count)

    def block_rows(h, r=0):
        return rows((ring(h, 0)[0] + r) % RING * block, block)

    def piece_rows(h, r=0):
        return rows((ring(h, 1)[0] + r) % RING * piece, piece)

    def own_piece(h):
        return rows(ring(h, 0)[0] * block + ring(h, 1)[0] * piece, piece)

    def copy(ar, h, stage, r):
        slot = ar * KVH + h
        if stage == 0:
            src, dst, phase = staged.at[slot, block_rows(h, r)], landed.at[slot, r - 1], 0
        elif stage == 1:
            src, dst, phase = partial.at[slot, piece_rows(h, r)], crossed.at[slot, r - 1], 1
        elif stage == 2:
            src = dst = gathered.at[slot, own_piece(h)]
            phase = 1
        else:
            src = dst = gathered.at[slot, block_rows(h)]
            phase = 0
        return pltpu.make_async_remote_copy(
            src_ref=src,
            dst_ref=dst,
            send_sem=send_sem.at[ar % 2, h, stage, r - 1],
            recv_sem=recv_sem.at[ar % 2, h, stage, r - 1],
            device_id=ring(h, phase)[1][r - 1],
            device_id_type=MESH,
        )

    def send(ar, h, stage):
        for r in range(1, RING):
            copy(ar, h, stage, r).start()

    def arrive(ar, h, stage):
        for r in range(1, RING):
            copy(ar, h, stage, r).wait()

    def first_sum(ar, h):
        arrive(ar, h, 0)
        slot = ar * KVH + h
        total = staged[slot, block_rows(h)].astype(jnp.float32)
        for r in range(1, RING):
            total = total + landed[slot, r - 1].astype(jnp.float32)
        partial[slot] = total.astype(jnp.bfloat16)
        send(ar, h, 1)

    def second_sum(ar, h):
        arrive(ar, h, 1)
        slot = ar * KVH + h
        total = partial[slot, piece_rows(h)].astype(jnp.float32)
        for r in range(1, RING):
            total = total + crossed[slot, r - 1].astype(jnp.float32)
        if ar % 2 == 0:
            total = jnp.concatenate([total[:, :HD], total[:, HD:] * VALUE_SCALE], axis=1)
        gathered[slot, own_piece(h)] = total.astype(jnp.bfloat16)
        send(ar, h, 2)

    def first_gather(ar, h):
        arrive(ar, h, 2)
        send(ar, h, 3)

    def key_cols(h):
        return pl.ds(h * HD, HD)

    def value_cols(h):
        return pl.ds(KVH * HD + h * HD, HD)

    def project(s, h, low):
        slot = 2 * s * KVH + h
        staged[slot] = lax.dot_general(
            tok_ref[s], low, (((0,), (0,)), ((), ())), preferred_element_type=jnp.float32
        ).astype(jnp.bfloat16)

    def prepare(s, h):
        for g in range(groups):
            cols = pl.ds((g * KVH + h) * HD, HD)
            q = query_ref[s, :, cols].astype(jnp.float32)
            norm = lax.rsqrt(jnp.mean(q * q, axis=-1, keepdims=True) + EPSILON)
            query_low[s, h, pl.ds(g * query_rows, query_rows)] = (q * norm).astype(jnp.bfloat16)
            cot[s, h, pl.ds(g * query_rows, query_rows)] = cot_in_ref[s, :, cols]

    def attend(s, h):
        slot = 2 * s * KVH + h
        q = query_low[s, h]
        c = cot[s, h]
        contract_last = (((1,), (1,)), ((), ()))
        position = first_row + lax.broadcasted_iota(jnp.int32, (block, lanes), 1) % query_rows
        row = lax.broadcasted_iota(jnp.int32, (block, lanes), 0)
        denom = jnp.zeros((1, lanes), jnp.float32)
        mixed = jnp.zeros((1, lanes), jnp.float32)
        for i in range(RING):
            part = pl.ds(i * block, block)
            keys = gathered[slot, part, :HD].astype(jnp.float32)
            norm = lax.rsqrt(jnp.mean(keys * keys, axis=-1, keepdims=True) + EPSILON)
            unit = keys * norm
            units[part] = unit
            norms[part] = jnp.broadcast_to(norm, unit.shape)
            scores = lax.dot_general(
                unit.astype(jnp.bfloat16), q, contract_last, preferred_element_type=jnp.float32
            )
            e = jnp.where(row + i * block <= position, jnp.exp(scores * HEAD_SCALE), 0.0)
            pg = lax.dot_general(
                gathered[slot, part, HD:], c, contract_last, preferred_element_type=jnp.float32
            )
            denom = denom + jnp.sum(e, axis=0, keepdims=True)
            mixed = mixed + jnp.sum(e * pg, axis=0, keepdims=True)
            raised[part] = e
            prob_grad[part] = pg
        inverse = 1.0 / denom
        mixed = mixed * inverse
        for r in (1, 2, 3, 0):
            part = block_rows(h, r)
            probs = raised[part] * inverse
            score_low = (probs * (prob_grad[part] - mixed) * HEAD_SCALE).astype(jnp.bfloat16)
            value_part = jnp.dot(probs.astype(jnp.bfloat16), c, preferred_element_type=jnp.float32)
            staged[slot + KVH, part, HD:] = value_part.astype(jnp.bfloat16)
            unit_grad = jnp.dot(score_low, q, preferred_element_type=jnp.float32)
            unit = units[part]
            key_part = (
                unit_grad - unit * jnp.mean(unit_grad * unit, axis=-1, keepdims=True)
            ) * norms[part]
            staged[slot + KVH, part, :HD] = key_part.astype(jnp.bfloat16)
            if r > 0:
                copy(2 * s + 1, h, 0, r).start()

    def descend(s, h):
        slot = (2 * s + 1) * KVH + h
        update = jnp.dot(tok_ref[s], gathered[slot], preferred_element_type=jnp.float32)
        scale = jnp.where(
            lax.broadcasted_iota(jnp.int32, (1, 2 * HD), 1) < HD, INNER_RATE, INNER_RATE * VALUE_SCALE
        )
        return theta[h] - update * scale

    def weights(h):
        return jnp.concatenate([w_ref[:, key_cols(h)], w_ref[:, value_cols(h)]], axis=1)

    def finish(h):
        low = weights(h).astype(jnp.float32)
        delta = (low - descend(STEPS - 1, h)).astype(jnp.bfloat16)
        payload = (PAIR_WEIGHT * low - DELTA_WEIGHT * delta.astype(jnp.float32)).astype(jnp.bfloat16)
        delta_ref[:, key_cols(h)] = delta[:, :HD]
        delta_ref[:, value_cols(h)] = delta[:, HD:]
        payload_ref[:, key_cols(h)] = payload[:, :HD]
        payload_ref[:, value_cols(h)] = payload[:, HD:]

    def task(h, index):
        ar, stage = index // 4, index % 4
        if stage == 0:
            if ar > 0:
                arrive(ar - 1, h, 3)
            s = ar // 2
            if ar == 2 * STEPS:
                finish(h)
                return
            if ar % 2 == 1:
                attend(s, h)
                return
            if s == 0:
                low = weights(h)
                theta[h] = low.astype(jnp.float32)
                project(0, h, low)
            else:
                new = descend(s - 1, h)
                theta[h] = new
                project(s, h, new.astype(jnp.bfloat16))
            if ar == 0 and h == 0:
                pl.semaphore_wait(barrier, 2 * (RING - 1))
            send(ar, h, 0)
            prepare(s, h)
        elif stage == 1:
            first_sum(ar, h)
        elif stage == 2:
            second_sum(ar, h)
        else:
            first_gather(ar, h)

    last = 8 * STEPS
    for tick in range(last + SKEW * (KVH - 1) + 1):
        for h in range(KVH):
            index = tick - SKEW * h
            if 0 <= index <= last:
                task(h, index)


def front(tokens, queries, cotangent, weights_low):
    steps, features, seq = tokens.shape
    columns = weights_low.shape[1]
    lanes = queries.shape[2] // (KVH * HD) * queries.shape[1]
    sums = 2 * steps * KVH
    vmem = pl.BlockSpec(memory_space=pltpu.VMEM)
    out = jax.ShapeDtypeStruct((features, columns), jnp.bfloat16)
    return pl.pallas_call(
        front_kernel,
        out_shape=(out, out),
        in_specs=[vmem] * 4,
        out_specs=(vmem, vmem),
        scratch_shapes=[
            pltpu.VMEM((KVH, features, 2 * HD), jnp.float32),
            pltpu.VMEM((sums, seq, 2 * HD), jnp.bfloat16),
            pltpu.VMEM((sums, seq, 2 * HD), jnp.bfloat16),
            pltpu.VMEM((sums, RING - 1, seq // RING, 2 * HD), jnp.bfloat16),
            pltpu.VMEM((sums, seq // RING, 2 * HD), jnp.bfloat16),
            pltpu.VMEM((sums, RING - 1, seq // RING // RING, 2 * HD), jnp.bfloat16),
            pltpu.VMEM((steps, KVH, lanes, HD), jnp.bfloat16),
            pltpu.VMEM((steps, KVH, lanes, HD), jnp.bfloat16),
            pltpu.VMEM((seq, lanes), jnp.float32),
            pltpu.VMEM((seq, lanes), jnp.float32),
            pltpu.VMEM((seq, HD), jnp.float32),
            pltpu.VMEM((seq, HD), jnp.float32),
            pltpu.SemaphoreType.DMA((2, KVH, 4, RING - 1)),
            pltpu.SemaphoreType.DMA((2, KVH, 4, RING - 1)),
        ],
        compiler_params=pltpu.CompilerParams(
            collective_id=0, has_side_effects=True, vmem_limit_bytes=40 * 1024 * 1024
        ),
    )(tokens, queries, cotangent, weights_low)


def from_partner(value, mask_value):
    replicas = lax.axis_size("rep")

    def by(mask, value):
        return lax.ppermute(value, "rep", [(source, source ^ mask) for source in range(replicas)])

    return lax.switch(mask_value - 1, [functools.partial(by, mask) for mask in range(1, replicas)], value)


def on_device(tokens, queries, cotangent, outer_weights, momentum, partner_mask):
    weights_low = outer_weights[0]
    momentum_low = momentum[0]
    payload, weight_delta = front(tokens[0], queries[0], cotangent[0], weights_low)
    partner_payload = from_partner(payload, partner_mask[0])
    outer_full = weights_low.astype(jnp.float32)
    step_change = (
        MOMENTUM_DECAY * momentum_low.astype(jnp.float32)
        - DELTA_WEIGHT * weight_delta.astype(jnp.float32)
        - PAIR_WEIGHT * outer_full
        + partner_payload.astype(jnp.float32)
    )
    return (
        (outer_full + step_change).astype(jnp.bfloat16)[None],
        step_change.astype(jnp.bfloat16)[None],
    )


def solution(mesh):
    in_specs = (
        P("rep", None, ("fsdp", "tp"), None),
        P("rep", None, "fsdp", "tp"),
        P("rep", None, "fsdp", "tp"),
        P("rep", ("fsdp", "tp"), None),
        P("rep", ("fsdp", "tp"), None),
        P(),
    )
    out_specs = (P("rep", ("fsdp", "tp"), None), P("rep", ("fsdp", "tp"), None))
    return jax.shard_map(
        on_device, mesh=mesh, in_specs=in_specs, out_specs=out_specs, check_vma=False
    )
```

time: 227 us -> 156 us (0.69)
  the two profiles are of different devices: /device:TPU:1 before, /device:TPU:384 now
where the time goes in v2:
time: 156 us
  Pallas kernels  90 us (58%)
  waiting for transfers between devices  52.1 us (33%)
  starting transfers between devices  5.08 us (3%)
  local copies, waits for them, and re-layouts  4.26 us (3%)
  other arithmetic  2.76 us (2%)
    pallas_call x1, Pallas kernels, front(): pl.pallas_call(front_kernel, out_shape=(out, out), in_specs=[vmem] * 4, o...  90 us
    ppermute x1, waiting for transfers between devices, by(): lax.ppermute(value, 'rep', [(source, source ^ mask) for source in range(r...  52.1 us
    ppermute x1, starting transfers between devices, by(): lax.ppermute(value, 'rep', [(source, source ^ mask) for source in range(r...  5.08 us
    unnamed x12, local copies, waits for them, and re-layouts  4.26 us
  transfers between devices with their start and end apart: 1, of which 1 were waited for; matrix products, arithmetic and copies ran while one was open for 0% of the time, Pallas kernels for 0%

profile of v2, /device:TPU:384, one launch (start us, length us, event | category | flops | bytes accessed | tf_op | source)
XLA Modules:
  0.0 155.6 jit_solution(16992952167879638496)
XLA Ops:
  1.3 0.0 copy-start
  1.3 1.1 copy-done
  2.4 0.0 copy-start.2
  2.4 1.1 copy-done.2
  3.5 0.0 copy-start.3
  3.5 1.0 copy-done.3
  4.5 0.0 copy-start.4
  4.5 1.0 copy-done.4
  5.5 0.0 copy-start.1
  5.5 0.0 copy-start.5
  5.5 90.0 %shard_map.77 = (bf16[320,1024]{1,0:T(8,128)(2,1)S(1)}, bf16[320,1024]{1,0:T(8,128)(2,1)S(1)}) custom-call(bf16[2,320,512]{2,1,0:T(8,128)(2,1)S(1)} %bitcast.20, bf16[2,64,2048]{2,1,0:T(8,128)(2,1)S(1)} %bitcast.21, bf16[2,64,2048]{2,1,0:T(8,128)(2,1)S(1)} %bitcast.22, bf16[320,1024]{1,0:T(8,128)(2,1)S(1)} %bitcast.19), custom_call_target="tpu_custom_call" | custom-call | tf_op jit(solution)/shard_map/pallas_call | solution.py:273
  95.6 57.2 %conditional.4 = (bf16[320,1024]{1,0:T(8,128)(2,1)}) conditional(s32[]{:T(128)} %bitcast.5, bf16[320,1024]{1,0:T(8,128)(2,1)S(1)} %get-tuple-element.74, bf16[320,1024]{1,0:T(8,128)(2,1)S(1)} %get-tuple-element.74, bf16[320,1024]{1,0:T(8,128)(2,1)S(1)} %get-tuple-element.74, ...), branch_computations={%region_0.0_spmd, %region_1.0_spmd, %region_2.0_spmd, %region_3.0_... | conditional | bytes 2621488
  95.6 5.1 %collective-permute-start.21 = (bf16[320,1024]{1,0:T(8,128)(2,1)S(1)}, bf16[320,1024]{1,0:T(8,128)(2,1)}, u32[]{:S(2)}, u32[]{:S(2)}) collective-permute-start(bf16[320,1024]{1,0:T(8,128)(2,1)S(1)} %param.21), channel_id=1, source_target_pairs={{0,352},{16,368},{32,320},{48,336},{64,288},{80,304},{96,256},{112... | collective-permute-start | bytes 1966088 | tf_op jit(solution)/shard_map/cond/branch_21_fun/ppermute | solution.py:304
  100.7 52.1 %collective-permute-done.21 = bf16[320,1024]{1,0:T(8,128)(2,1)} collective-permute-done((bf16[320,1024]{1,0:T(8,128)(2,1)S(1)}, bf16[320,1024]{1,0:T(8,128)(2,1)}, u32[]{:S(2)}, u32[]{:S(2)}) %collective-permute-start.21) | collective-permute-done | bytes 655392 | tf_op jit(solution)/shard_map/cond/branch_21_fun/ppermute | solution.py:304
  152.8 0.0 copy-done.1
  152.8 0.0 copy-done.5
  152.8 2.8 %convert_bitcast_fusion = (bf16[1,320,1024]{2,1,0:T(8,128)(2,1)}, bf16[1,320,1024]{2,1,0:T(8,128)(2,1)}) fusion(bf16[320,1024]{1,0:T(8,128)(2,1)} %get-tuple-element.77, bf16[320,1024]{1,0:T(8,128)(2,1)S(1)} %get-tuple-element.73, bf16[1,320,1024]{2,1,0:T(8,128)(2,1)S(1)} %copy-done.5, bf16[1,320,1024]{2,1,0:T(8,128)(2,1)S(1)} %copy-done.1), kind=kLoop, calls=%fused_computation.7 | loop fusion | flops 4259840 | bytes 3932160 | tf_op jit(solution)/shard_map/broadcast_in_dim | solution.py:323
Async XLA Ops:
  1.3 1.1 copy-start
  2.4 1.1 copy-start.2
  3.5 1.0 copy-start.3
  4.5 1.0 copy-start.4
  5.5 147.3 %copy-start.1 = (bf16[1,320,1024]{2,1,0:T(8,128)(2,1)S(1)}, bf16[1,320,1024]{2,1,0:T(8,128)(2,1)}, u32[]{:S(2)}) copy-start(bf16[1,320,1024]{2,1,0:T(8,128)(2,1)} %param.40) | copy-start | bytes 1966084
  5.5 147.3 %copy-start.5 = (bf16[1,320,1024]{2,1,0:T(8,128)(2,1)S(1)}, bf16[1,320,1024]{2,1,0:T(8,128)(2,1)}, u32[]{:S(2)}) copy-start(bf16[1,320,1024]{2,1,0:T(8,128)(2,1)} %param.41) | copy-start | bytes 1966084
  95.6 57.2 %collective-permute-start.21 = (bf16[320,1024]{1,0:T(8,128)(2,1)S(1)}, bf16[320,1024]{1,0:T(8,128)(2,1)}, u32[]{:S(2)}, u32[]{:S(2)}) collective-permute-start(bf16[320,1024]{1,0:T(8,128)(2,1)S(1)} %param.21), channel_id=1, source_target_pairs={{0,352},{16,368},{32,320},{48,336},{64,288},{80,304},{96,256},{112... | collective-permute-start | bytes 1966088 | tf_op jit(solution)/shard_map/cond/branch_21_fun/ppermute | solution.py:304

commit v3 on v2

--- a/solution.py
+++ b/solution.py
@@ -22,6 +22,7 @@
 MESH = pl.DeviceIdType.MESH
 RING = 4
 SKEW = 0
+FAR_FIRST = (2, 1, 3)
 VALUE_SCALE = D ** (-0.5)
 HEAD_SCALE = HD ** (-0.5)
 
@@ -37,12 +38,16 @@
 
 
 def front_kernel(
+    tok_hbm,
+    query_hbm,
+    cot_hbm,
+    w_hbm,
+    payload_ref,
+    delta_ref,
     tok_ref,
     query_ref,
     cot_in_ref,
     w_ref,
-    payload_ref,
-    delta_ref,
     theta,
     gathered,
     staged,
@@ -55,6 +60,7 @@
     prob_grad,
     units,
     norms,
+    load_sem,
     send_sem,
     recv_sem,
 ):
@@ -63,9 +69,15 @@
     groups = query_ref.shape[2] // (KVH * HD)
     lanes = groups * query_rows
     block = seq // RING
-    piece = block // RING
     rings = [ring_ids(0), ring_ids(1)]
     first_row = lax.axis_index("fsdp") * query_rows
+
+    pairs = [(w_hbm, w_ref)]
+    for s in range(STEPS):
+        pairs += [(a.at[s], b.at[s]) for a, b in ((tok_hbm, tok_ref), (query_hbm, query_ref), (cot_hbm, cot_in_ref))]
+    loads = [pltpu.make_async_copy(a, b, load_sem.at[i]) for i, (a, b) in enumerate(pairs)]
+    for load in loads:
+        load.start()
 
     barrier = pltpu.get_barrier_semaphore()
     for _, ids in rings:
@@ -75,27 +87,15 @@
     def ring(h, phase):
         return rings[(h + phase) % 2]
 
-    def rows(start, count):
-        return pl.ds(pl.multiple_of(start, piece), count)
-
     def block_rows(h, r=0):
-        return rows((ring(h, 0)[0] + r) % RING * block, block)
-
-    def piece_rows(h, r=0):
-        return rows((ring(h, 1)[0] + r) % RING * piece, piece)
-
-    def own_piece(h):
-        return rows(ring(h, 0)[0] * block + ring(h, 1)[0] * piece, piece)
+        return pl.ds(pl.multiple_of((ring(h, 0)[0] + r) % RING * block, block), block)
 
     def copy(ar, h, stage, r):
         slot = ar * KVH + h
         if stage == 0:
             src, dst, phase = staged.at[slot, block_rows(h, r)], landed.at[slot, r - 1], 0
         elif stage == 1:
-            src, dst, phase = partial.at[slot, piece_rows(h, r)], crossed.at[slot, r - 1], 1
-        elif stage == 2:
-            src = dst = gathered.at[slot, own_piece(h)]
-            phase = 1
+            src, dst, phase = partial.at[slot], crossed.at[slot, r - 1], 1
         else:
             src = dst = gathered.at[slot, block_rows(h)]
             phase = 0
@@ -109,7 +109,7 @@
         )
 
     def send(ar, h, stage):
-        for r in range(1, RING):
+        for r in FAR_FIRST:
             copy(ar, h, stage, r).start()
 
     def arrive(ar, h, stage):
@@ -128,17 +128,13 @@
     def second_sum(ar, h):
         arrive(ar, h, 1)
         slot = ar * KVH + h
-        total = partial[slot, piece_rows(h)].astype(jnp.float32)
+        total = partial[slot].astype(jnp.float32)
         for r in range(1, RING):
             total = total + crossed[slot, r - 1].astype(jnp.float32)
         if ar % 2 == 0:
             total = jnp.concatenate([total[:, :HD], total[:, HD:] * VALUE_SCALE], axis=1)
-        gathered[slot, own_piece(h)] = total.astype(jnp.bfloat16)
+        gathered[slot, block_rows(h)] = total.astype(jnp.bfloat16)
         send(ar, h, 2)
-
-    def first_gather(ar, h):
-        arrive(ar, h, 2)
-        send(ar, h, 3)
 
     def key_cols(h):
         return pl.ds(h * HD, HD)
@@ -189,7 +185,7 @@
             prob_grad[part] = pg
         inverse = 1.0 / denom
         mixed = mixed * inverse
-        for r in (1, 2, 3, 0):
+        for r in FAR_FIRST + (0,):
             part = block_rows(h, r)
             probs = raised[part] * inverse
             score_low = (probs * (prob_grad[part] - mixed) * HEAD_SCALE).astype(jnp.bfloat16)
@@ -225,10 +221,10 @@
         payload_ref[:, value_cols(h)] = payload[:, HD:]
 
     def task(h, index):
-        ar, stage = index // 4, index % 4
+        ar, stage = index // 3, index % 3
         if stage == 0:
             if ar > 0:
-                arrive(ar - 1, h, 3)
+                arrive(ar - 1, h, 2)
             s = ar // 2
             if ar == 2 * STEPS:
                 finish(h)
@@ -236,6 +232,10 @@
             if ar % 2 == 1:
                 attend(s, h)
                 return
+            if h == 0:
+                if s == 0:
+                    loads[0].wait()
+                loads[3 * s + 1].wait()
             if s == 0:
                 low = weights(h)
                 theta[h] = low.astype(jnp.float32)
@@ -247,15 +247,17 @@
             if ar == 0 and h == 0:
                 pl.semaphore_wait(barrier, 2 * (RING - 1))
             send(ar, h, 0)
-            prepare(s, h)
+            if h == 1:
+                loads[3 * s + 2].wait()
+                loads[3 * s + 3].wait()
+                for other in range(KVH):
+                    prepare(s, other)
         elif stage == 1:
             first_sum(ar, h)
-        elif stage == 2:
+        else:
             second_sum(ar, h)
-        else:
-            first_gather(ar, h)
-
-    last = 8 * STEPS
+
+    last = 6 * STEPS
     for tick in range(last + SKEW * (KVH - 1) + 1):
         for h in range(KVH):
             index = tick - SKEW * h
@@ -273,26 +275,31 @@
     return pl.pallas_call(
         front_kernel,
         out_shape=(out, out),
-        in_specs=[vmem] * 4,
+        in_specs=[pl.BlockSpec(memory_space=pl.ANY)] * 4,
         out_specs=(vmem, vmem),
         scratch_shapes=[
+            pltpu.VMEM(tokens.shape, tokens.dtype),
+            pltpu.VMEM(queries.shape, queries.dtype),
+            pltpu.VMEM(cotangent.shape, cotangent.dtype),
+            pltpu.VMEM(weights_low.shape, weights_low.dtype),
             pltpu.VMEM((KVH, features, 2 * HD), jnp.float32),
             pltpu.VMEM((sums, seq, 2 * HD), jnp.bfloat16),
             pltpu.VMEM((sums, seq, 2 * HD), jnp.bfloat16),
             pltpu.VMEM((sums, RING - 1, seq // RING, 2 * HD), jnp.bfloat16),
             pltpu.VMEM((sums, seq // RING, 2 * HD), jnp.bfloat16),
-            pltpu.VMEM((sums, RING - 1, seq // RING // RING, 2 * HD), jnp.bfloat16),
+            pltpu.VMEM((sums, RING - 1, seq // RING, 2 * HD), jnp.bfloat16),
             pltpu.VMEM((steps, KVH, lanes, HD), jnp.bfloat16),
             pltpu.VMEM((steps, KVH, lanes, HD), jnp.bfloat16),
             pltpu.VMEM((seq, lanes), jnp.float32),
             pltpu.VMEM((seq, lanes), jnp.float32),
             pltpu.VMEM((seq, HD), jnp.float32),
             pltpu.VMEM((seq, HD), jnp.float32),
-            pltpu.SemaphoreType.DMA((2, KVH, 4, RING - 1)),
-            pltpu.SemaphoreType.DMA((2, KVH, 4, RING - 1)),
+            pltpu.SemaphoreType.DMA((3 * STEPS + 1,)),
+            pltpu.SemaphoreType.DMA((2, KVH, 3, RING - 1)),
+            pltpu.SemaphoreType.DMA((2, KVH, 3, RING - 1)),
         ],
         compiler_params=pltpu.CompilerParams(
-            collective_id=0, has_side_effects=True, vmem_limit_bytes=40 * 1024 * 1024
+            collective_id=0, has_side_effects=True, vmem_limit_bytes=60 * 1024 * 1024
         ),
     )(tokens, queries, cotangent, weights_low)
 

time: 156 us -> 156 us (level)
  the two profiles are of different devices: /device:TPU:384 before, /device:TPU:160 now
where the time goes in v3:
time: 156 us
  Pallas kernels  84.6 us (54%)
  waiting for transfers between devices  65.1 us (42%)
  other arithmetic  2.95 us (2%)
  starting transfers between devices  2.19 us (1%)
    pallas_call x1, Pallas kernels, front(): pl.pallas_call(front_kernel, out_shape=(out, out), in_specs=[pl.BlockSpec...  84.6 us
    ppermute x1, waiting for transfers between devices, by(): lax.ppermute(value, 'rep', [(source, source ^ mask) for source in range(r...  65.1 us
  transfers between devices with their start and end apart: 1, of which 1 were waited for; matrix products, arithmetic and copies ran while one was open for 0% of the time, Pallas kernels for 0%

profile of v3, /device:TPU:160, one launch (start us, length us, event | category | flops | bytes accessed | tf_op | source)
XLA Modules:
  0.0 156.2 jit_solution(8719334081553903764)
XLA Ops:
  1.3 0.0 copy-start
  1.3 0.0 copy-start.1
  1.3 84.6 %shard_map.77 = (bf16[320,1024]{1,0:T(8,128)(2,1)S(1)}, bf16[320,1024]{1,0:T(8,128)(2,1)}) custom-call(bf16[2,320,512]{2,1,0:T(8,128)(2,1)} %bitcast.20, bf16[2,64,2048]{2,1,0:T(8,128)(2,1)} %bitcast.21, bf16[2,64,2048]{2,1,0:T(8,128)(2,1)} %bitcast.22, bf16[320,1024]{1,0:T(8,128)(2,1)} %bitcast.19), custom_call_target="tpu_custom_call" | custom-call | tf_op jit(solution)/shard_map/pallas_call | solution.py:275
  85.9 67.4 %conditional.4 = (bf16[320,1024]{1,0:T(8,128)(2,1)}) conditional(s32[]{:T(128)} %bitcast.5, bf16[320,1024]{1,0:T(8,128)(2,1)S(1)} %get-tuple-element.74, bf16[320,1024]{1,0:T(8,128)(2,1)S(1)} %get-tuple-element.74, bf16[320,1024]{1,0:T(8,128)(2,1)S(1)} %get-tuple-element.74, ...), branch_computations={%region_0.0_spmd, %region_1.0_spmd, %region_2.0_spmd, %region_3.0_... | conditional | bytes 2621488
  85.9 2.2 %collective-permute-start.18 = (bf16[320,1024]{1,0:T(8,128)(2,1)S(1)}, bf16[320,1024]{1,0:T(8,128)(2,1)}, u32[]{:S(2)}, u32[]{:S(2)}) collective-permute-start(bf16[320,1024]{1,0:T(8,128)(2,1)S(1)} %param.18), channel_id=1, source_target_pairs={{0,304},{16,288},{32,272},{48,256},{64,368},{80,352},{96,336},{112... | collective-permute-start | bytes 1966088 | tf_op jit(solution)/shard_map/cond/branch_18_fun/ppermute | solution.py:311
  88.1 65.1 %collective-permute-done.18 = bf16[320,1024]{1,0:T(8,128)(2,1)} collective-permute-done((bf16[320,1024]{1,0:T(8,128)(2,1)S(1)}, bf16[320,1024]{1,0:T(8,128)(2,1)}, u32[]{:S(2)}, u32[]{:S(2)}) %collective-permute-start.18) | collective-permute-done | bytes 655392 | tf_op jit(solution)/shard_map/cond/branch_18_fun/ppermute | solution.py:311
  153.3 0.0 copy-done
  153.3 0.0 copy-done.1
  153.3 3.0 %convert_bitcast_fusion = (bf16[1,320,1024]{2,1,0:T(8,128)(2,1)}, bf16[1,320,1024]{2,1,0:T(8,128)(2,1)}) fusion(bf16[320,1024]{1,0:T(8,128)(2,1)} %get-tuple-element.77, bf16[320,1024]{1,0:T(8,128)(2,1)} %get-tuple-element.73, bf16[1,320,1024]{2,1,0:T(8,128)(2,1)S(1)} %copy-done.1, bf16[1,320,1024]{2,1,0:T(8,128)(2,1)S(1)} %copy-done), kind=kLoop, calls=%fused_computation.7 | loop fusion | flops 4259840 | bytes 3932160 | tf_op jit(solution)/shard_map/broadcast_in_dim | solution.py:330
Async XLA Ops:
  1.3 152.0 %copy-start = (bf16[1,320,1024]{2,1,0:T(8,128)(2,1)S(1)}, bf16[1,320,1024]{2,1,0:T(8,128)(2,1)}, u32[]{:S(2)}) copy-start(bf16[1,320,1024]{2,1,0:T(8,128)(2,1)} %param.40) | copy-start | bytes 1966084
  1.3 152.0 %copy-start.1 = (bf16[1,320,1024]{2,1,0:T(8,128)(2,1)S(1)}, bf16[1,320,1024]{2,1,0:T(8,128)(2,1)}, u32[]{:S(2)}) copy-start(bf16[1,320,1024]{2,1,0:T(8,128)(2,1)} %param.41) | copy-start | bytes 1966084
  85.9 67.3 %collective-permute-start.18 = (bf16[320,1024]{1,0:T(8,128)(2,1)S(1)}, bf16[320,1024]{1,0:T(8,128)(2,1)}, u32[]{:S(2)}, u32[]{:S(2)}) collective-permute-start(bf16[320,1024]{1,0:T(8,128)(2,1)S(1)} %param.18), channel_id=1, source_target_pairs={{0,304},{16,288},{32,272},{48,256},{64,368},{80,352},{96,336},{112... | collective-permute-start | bytes 1966088 | tf_op jit(solution)/shard_map/cond/branch_18_fun/ppermute | solution.py:311

commit v4 on v3

--- a/solution.py
+++ b/solution.py
@@ -304,12 +304,41 @@
     )(tokens, queries, cotangent, weights_low)
 
 
+def swap_kernel(mask, payload_ref, partner_ref, send_sem, recv_sem):
+    other = lax.axis_index("rep")
+    for bit in range(lax.axis_size("rep").bit_length() - 1):
+        if mask >> bit & 1:
+            other = other + (1 - 2 * (lax.axis_index("rep") // 2**bit % 2)) * 2**bit
+    partner = (other, lax.axis_index("fsdp"), lax.axis_index("tp"))
+    barrier = pltpu.get_barrier_semaphore()
+    pl.semaphore_signal(barrier, inc=1, device_id=partner, device_id_type=MESH)
+    pl.semaphore_wait(barrier, 1)
+    copy = pltpu.make_async_remote_copy(
+        src_ref=payload_ref,
+        dst_ref=partner_ref,
+        send_sem=send_sem,
+        recv_sem=recv_sem,
+        device_id=partner,
+        device_id_type=MESH,
+    )
+    copy.start()
+    copy.wait()
+
+
 def from_partner(value, mask_value):
+    space = pl.BlockSpec(memory_space=pl.ANY)
+
+    def by(mask, value):
+        return pl.pallas_call(
+            functools.partial(swap_kernel, mask),
+            out_shape=jax.ShapeDtypeStruct(value.shape, value.dtype),
+            in_specs=[space],
+            out_specs=space,
+            scratch_shapes=[pltpu.SemaphoreType.DMA, pltpu.SemaphoreType.DMA],
+            compiler_params=pltpu.CompilerParams(collective_id=mask, has_side_effects=True),
+        )(value)
+
     replicas = lax.axis_size("rep")
-
-    def by(mask, value):
-        return lax.ppermute(value, "rep", [(source, source ^ mask) for source in range(replicas)])
-
     return lax.switch(mask_value - 1, [functools.partial(by, mask) for mask in range(1, replicas)], value)
 
 

time: 156 us -> 149 us (0.955)
  the two profiles are of different devices: /device:TPU:160 before, /device:TPU:1 now
where the time goes in v4:
time: 149 us; the launch traced here: 148 us
  Pallas kernels  145 us (97%)
  other arithmetic  1.69 us (1%)
    pallas_call x1, Pallas kernels, front(): pl.pallas_call(front_kernel, out_shape=(out, out), in_specs=[pl.BlockSpec...  77.3 us
    pallas_call x1, Pallas kernels, by(): pl.pallas_call(functools.partial(swap_kernel, mask), out_shape=jax.ShapeD...  67.5 us

profile of v4, /device:TPU:1, one launch (start us, length us, event | category | flops | bytes accessed | tf_op | source)
XLA Modules:
  0.0 147.9 jit_solution(15631079529005473595)
XLA Ops:
  1.3 77.3 %shard_map.77 = (bf16[320,1024]{1,0:T(8,128)(2,1)S(1)}, bf16[320,1024]{1,0:T(8,128)(2,1)}) custom-call(bf16[2,320,512]{2,1,0:T(8,128)(2,1)} %bitcast.20, bf16[2,64,2048]{2,1,0:T(8,128)(2,1)} %bitcast.21, bf16[2,64,2048]{2,1,0:T(8,128)(2,1)} %bitcast.22, bf16[320,1024]{1,0:T(8,128)(2,1)} %bitcast.19), custom_call_target="tpu_custom_call" | custom-call | tf_op jit(solution)/shard_map/pallas_call | solution.py:275
  78.6 0.0 copy-start
  78.6 0.0 copy-start.1
  78.6 0.0 copy-start.2
  78.6 67.6 %conditional.4 = (bf16[320,1024]{1,0:T(8,128)(2,1)S(1)}) conditional(s32[]{:T(128)} %bitcast.5, bf16[320,1024]{1,0:T(8,128)(2,1)S(1)} %get-tuple-element.74, bf16[320,1024]{1,0:T(8,128)(2,1)S(1)} %get-tuple-element.74, bf16[320,1024]{1,0:T(8,128)(2,1)S(1)} %get-tuple-element.74, ...), branch_computations={%region_0.0_spmd, %region_1.0_spmd, %region_2.0_spmd, %region_3.0_... | conditional | bytes 8
  78.7 67.5 %branch_25_fun.1 = bf16[320,1024]{1,0:T(8,128)(2,1)S(1)} custom-call(bf16[320,1024]{1,0:T(8,128)(2,1)S(1)} %payload_ref.25), custom_call_target="tpu_custom_call" | custom-call | tf_op jit(solution)/shard_map/cond/branch_25_fun/pallas_call | solution.py:332
  146.2 0.0 copy-done
  146.2 0.0 copy-done.1
  146.2 0.0 copy-done.2
  146.3 1.7 %convert_bitcast_fusion = (bf16[1,320,1024]{2,1,0:T(8,128)(2,1)}, bf16[1,320,1024]{2,1,0:T(8,128)(2,1)}) fusion(bf16[320,1024]{1,0:T(8,128)(2,1)S(1)} %get-tuple-element.77, bf16[320,1024]{1,0:T(8,128)(2,1)S(1)} %copy-done.2, bf16[1,320,1024]{2,1,0:T(8,128)(2,1)S(1)} %copy-done.1, bf16[1,320,1024]{2,1,0:T(8,128)(2,1)S(1)} %copy-done), kind=kLoop, calls=%fused_computation.7 | loop fusion | flops 4259840 | bytes 3932160 | tf_op jit(solution)/shard_map/broadcast_in_dim | solution.py:359
Async XLA Ops:
  78.6 67.6 %copy-start = (bf16[1,320,1024]{2,1,0:T(8,128)(2,1)S(1)}, bf16[1,320,1024]{2,1,0:T(8,128)(2,1)}, u32[]{:S(2)}) copy-start(bf16[1,320,1024]{2,1,0:T(8,128)(2,1)} %param.40) | copy-start | bytes 1966084
  78.6 67.6 %copy-start.1 = (bf16[1,320,1024]{2,1,0:T(8,128)(2,1)S(1)}, bf16[1,320,1024]{2,1,0:T(8,128)(2,1)}, u32[]{:S(2)}) copy-start(bf16[1,320,1024]{2,1,0:T(8,128)(2,1)} %param.41) | copy-start | bytes 1966084
  78.6 67.6 %copy-start.2 = (bf16[320,1024]{1,0:T(8,128)(2,1)S(1)}, bf16[320,1024]{1,0:T(8,128)(2,1)}, u32[]{:S(2)}) copy-start(bf16[320,1024]{1,0:T(8,128)(2,1)} %get-tuple-element.73) | copy-start | bytes 1966084
